TPU v7x, 32 devices: a whole 2x2x4 slice. The times are simulated.
32 devices in a mesh: leaf: 16 (over z, y, x), col: 2 (over core).
Axes of the slice: x: 2, y: 2, z: 4, core: 2. Of those that a mesh axis runs over, the one named last changes fastest.
Arguments:
- rows_a: bfloat16 [32768, 1024], P(('leaf', 'col')), may hold values from -0.125 to 0.125
- stair_counts: int32 [16, 8], P('leaf'), may hold values from 192 to 448, as said below
- block_maps: int32 [4, 8, 2, 2, 16], replicated, may hold values from 0 to 19, as said below
Outputs:
- factor: float32 [4, 16, 1280, 256], P(None, 'leaf', 'col')
- contribution: float32 [16, 1024, 1024], P('leaf', 'col')
Inputs may be any that keep to these rules, and one draw needn't show every extreme that they name: Each row of stair_counts sums to 2048; in every row one count equals 192 and one equals 448. `block_maps`: for each level, front, child and index of col the 16 entries are distinct, and those of the two children together name every value below 20.
All inputs are finite; a program needn't handle non-finite values.
Results may differ from a plain program's by a relative error of at most 0.0003.
Values sent between devices are 32-bit elements; how exact they have to be, the bound alone decides.
A program may use at most 128 MiB of HBM per device.

v0:
```python
import jax
import jax.numpy as jnp
from jax import lax
from jax.sharding import PartitionSpec as P

KP = 256
SB = 32
LEVELS = 4


def swapped(value, axis, stride):
    mask = 2**stride
    pairs = [(source, source ^ mask) for source in range(lax.axis_size(axis))]
    return lax.ppermute(value, axis, pairs)


def place_child(child, child_maps, col_index, sub_count, sub_width):
    col_count, child_subs = child_maps.shape
    matches = (child_maps[:, :, None] == lax.iota(jnp.int32, sub_count)[None, None, :]).astype(
        jnp.int32
    )
    source = jnp.sum(matches * lax.iota(jnp.int32, child_subs)[None, :, None], axis=1)
    present = jnp.sum(matches, axis=1)
    within = lax.iota(jnp.int32, sub_width)
    strip_size = child_subs * sub_width
    column_source = (
        lax.iota(jnp.int32, col_count)[:, None, None] * strip_size
        + source[:, :, None] * sub_width
        + within[None, None, :]
    ).reshape(-1)
    column_live = jnp.broadcast_to(present[:, :, None], (col_count, sub_count, sub_width)).reshape(
        -1
    )
    own_source = lax.dynamic_index_in_dim(source, col_index, 0, keepdims=False)
    own_present = lax.dynamic_index_in_dim(present, col_index, 0, keepdims=False)
    row_source = (own_source[:, None] * sub_width + within[None, :]).reshape(-1)
    row_live = jnp.broadcast_to(own_present[:, None], (sub_count, sub_width)).reshape(-1)
    picked = jnp.take(jnp.take(child, row_source, axis=0), column_source, axis=1)
    keep = (row_live[:, None] > 0) & (column_live[None, :] > 0)
    return jnp.where(keep, picked, jnp.zeros_like(picked))


def body(rows_a, stair_counts, block_maps):
    col_count = lax.axis_size("col")
    col_index = lax.axis_index("col")
    leaf_index = lax.axis_index("leaf")
    local_rows, width = rows_a.shape
    strip_rows = width // col_count
    pivot_share = KP // col_count
    front_cols = strip_rows + pivot_share
    sub_count = front_cols // SB
    bounds = jnp.cumsum(stair_counts[0])
    row_index = col_index * local_rows + lax.iota(jnp.int32, local_rows)
    leading = jnp.sum((bounds[None, :] <= row_index[:, None]).astype(jnp.int32), axis=1)
    column_block = lax.iota(jnp.int32, width) // (width // stair_counts.shape[1])
    masked = jnp.where(column_block[None, :] >= leading[:, None], rows_a, jnp.zeros_like(rows_a))
    current = lax.psum_scatter(
        lax.dot_general(
            masked, masked, (((0,), (0,)), ((), ())), preferred_element_type=jnp.float32
        ),
        "col",
        scatter_dimension=0,
        tiled=True,
    )
    factors = []
    for level_index in range(LEVELS):
        partner = swapped(current, "leaf", level_index)
        pair_bit = leaf_index >> level_index & 1
        is_lower = pair_bit == 0
        first_child = jnp.where(is_lower, current, partner)
        second_child = jnp.where(is_lower, partner, current)
        front_maps = lax.dynamic_index_in_dim(
            block_maps[level_index], leaf_index >> level_index + 1, 0, keepdims=False
        )
        assembled = place_child(first_child, front_maps[0], col_index, sub_count, SB) + place_child(
            second_child, front_maps[1], col_index, sub_count, SB
        )
        by_device = assembled.reshape(front_cols, col_count, front_cols)
        pivot_cols = by_device[:, :, :pivot_share].reshape(front_cols, col_count * pivot_share)
        rest_cols = by_device[:, :, pivot_share:].reshape(front_cols, col_count * strip_rows)
        pivot_block = lax.all_gather(pivot_cols[:pivot_share], "col", axis=0, tiled=True)
        lower_factor = jnp.linalg.cholesky(pivot_block)
        coupling = pivot_cols[pivot_share:]
        upper_rows = jax.scipy.linalg.solve_triangular(lower_factor, coupling.T, lower=True).T
        own_lower = lax.dynamic_slice_in_dim(lower_factor, col_index * pivot_share, pivot_share, 0)
        factors.append(jnp.concatenate([own_lower, upper_rows], axis=0))
        corner = rest_cols[pivot_share:]
        product = lax.dot_general(
            upper_rows,
            lax.all_gather(upper_rows, "col", axis=0, tiled=True),
            (((1,), (1,)), ((), ())),
            precision=lax.Precision.HIGHEST,
            preferred_element_type=jnp.float32,
        )
        current = corner - product
    factor = jnp.stack(factors)[:, None]
    return (factor, current[None])


def solution(mesh):
    return jax.shard_map(
        body,
        mesh=mesh,
        in_specs=(P(("leaf", "col"), None), P("leaf", None), P()),
        out_specs=(P(None, "leaf", "col", None), P("leaf", "col", None)),
        check_vma=False,
    )
```

profile of v0, /device:TPU:0, one launch (start us, length us, event | category | flops | bytes accessed | tf_op | source)
XLA Modules:
  0.0 812.9 jit_solution(9978441971090246161)
XLA Ops:
  8.2 6.8 fusion.4
  19.9 10.1 %reduce-scatter.2.cloned.1.call-done = f32[512,1024]{1,0:T(8,128)} async-done(((f32[1024,1024]{1,0:T(8,128)}), f32[512,1024]{1,0:T(8,128)}) %reduce-scatter.2.cloned.1.call-update) | async-done | bytes 2097168 | tf_op jit(solution)/shard_map/reduce_scatter | solution.py:57
  33.4 44.7 %collective-permute-done = f32[512,1024]{1,0:T(8,128)} collective-permute-done((f32[512,1024]{1,0:T(8,128)}, f32[512,1024]{1,0:T(8,128)}, u32[]{:S(2)}, u32[]{:S(2)}) %collective-permute-start) | collective-permute-done | bytes 2097184 | tf_op jit(solution)/shard_map/ppermute | solution.py:14
  78.2 4.2 broadcast_select_fusion.15
  91.4 6.1 gather_fusion.2
  104.2 4.8 gather_fusion.1
  109.1 7.2 gather_fusion.3
  124.7 11.7 %cholesky.214 = f32[128,128]{1,0:T(8,128)S(1)} custom-call(f32[128,128]{1,0:T(8,128)S(1)} %cholesky.346), custom_call_target="Cholesky" | custom-call | tf_op jit(solution)/shard_map/jit(cholesky)/cholesky | solution.py:82
  137.1 9.8 %custom-call.17 = f32[1,128,128]{1,2,0:T(8,128)S(1)} custom-call(f32[1,128,128]{2,1,0:T(8,128)S(1)} %get-tuple-element.133), custom_call_target="InvertDiagBlocksLowerTriangular" | custom-call | tf_op jit(solution)/shard_map/jit(cholesky)/cholesky | solution.py:82
  147.4 11.7 %cholesky.231 = f32[128,128]{1,0:T(8,128)S(1)} custom-call(f32[128,128]{1,0:T(8,128)S(1)} %convolution_subtract_fusion.10), custom_call_target="Cholesky" | custom-call | tf_op jit(solution)/shard_map/jit(cholesky)/cholesky | solution.py:82
  164.3 5.4 while.8
  169.7 21.2 %custom-call.18 = f32[2,128,128]{1,2,0:T(8,128)} custom-call(f32[2,128,128]{2,1,0:T(8,128)} %get-tuple-element.32), custom_call_target="InvertDiagBlocksLowerTriangular" | custom-call | tf_op jit(solution)/shard_map/jit(_solve_triangular)/triangular_solve | solution.py:84
  206.8 4.4 convolution_subtract_fusion.2
  213.5 45.8 %collective-permute-done.1 = f32[512,1024]{1,0:T(8,128)} collective-permute-done((f32[512,1024]{1,0:T(8,128)}, f32[512,1024]{1,0:T(8,128)}, u32[]{:S(2)}, u32[]{:S(2)}) %collective-permute-start.1) | collective-permute-done | bytes 2097184 | tf_op jit(solution)/shard_map/ppermute | solution.py:14
  259.4 4.2 broadcast_select_fusion.13
  272.6 6.1 gather_fusion.6
  285.4 4.8 gather_fusion.5
  290.3 7.2 gather_fusion.7
  297.5 3.5 fusion.2
  305.9 11.7 %cholesky.248 = f32[128,128]{1,0:T(8,128)S(1)} custom-call(f32[128,128]{1,0:T(8,128)S(1)} %cholesky.349), custom_call_target="Cholesky" | custom-call | tf_op jit(solution)/shard_map/jit(cholesky)/cholesky | solution.py:82
  318.3 9.8 %custom-call.19 = f32[1,128,128]{1,2,0:T(8,128)S(1)} custom-call(f32[1,128,128]{2,1,0:T(8,128)S(1)} %get-tuple-element.129), custom_call_target="InvertDiagBlocksLowerTriangular" | custom-call | tf_op jit(solution)/shard_map/jit(cholesky)/cholesky | solution.py:82
  328.6 11.7 %cholesky.265 = f32[128,128]{1,0:T(8,128)S(1)} custom-call(f32[128,128]{1,0:T(8,128)S(1)} %convolution_subtract_fusion.9), custom_call_target="Cholesky" | custom-call | tf_op jit(solution)/shard_map/jit(cholesky)/cholesky | solution.py:82
  344.7 5.3 while.9
  350.1 21.1 %custom-call.20 = f32[2,128,128]{1,2,0:T(8,128)} custom-call(f32[2,128,128]{2,1,0:T(8,128)} %get-tuple-element.33), custom_call_target="InvertDiagBlocksLowerTriangular" | custom-call | tf_op jit(solution)/shard_map/jit(_solve_triangular)/triangular_solve | solution.py:84
  387.2 4.4 convolution_subtract_fusion.1
  393.9 45.8 %collective-permute-done.2 = f32[512,1024]{1,0:T(8,128)} collective-permute-done((f32[512,1024]{1,0:T(8,128)}, f32[512,1024]{1,0:T(8,128)}, u32[]{:S(2)}, u32[]{:S(2)}) %collective-permute-start.2) | collective-permute-done | bytes 2097184 | tf_op jit(solution)/shard_map/ppermute | solution.py:14
  439.8 4.2 broadcast_select_fusion.11
  453.0 6.1 gather_fusion.10
  465.8 4.8 gather_fusion.9
  470.7 7.2 gather_fusion.11
  486.5 11.7 %cholesky.282 = f32[128,128]{1,0:T(8,128)S(1)} custom-call(f32[128,128]{1,0:T(8,128)S(1)} %cholesky.352), custom_call_target="Cholesky" | custom-call | tf_op jit(solution)/shard_map/jit(cholesky)/cholesky | solution.py:82
  498.9 9.8 %custom-call.21 = f32[1,128,128]{1,2,0:T(8,128)S(1)} custom-call(f32[1,128,128]{2,1,0:T(8,128)S(1)} %get-tuple-element.125), custom_call_target="InvertDiagBlocksLowerTriangular" | custom-call | tf_op jit(solution)/shard_map/jit(cholesky)/cholesky | solution.py:82
  509.3 11.7 %cholesky.299 = f32[128,128]{1,0:T(8,128)S(1)} custom-call(f32[128,128]{1,0:T(8,128)S(1)} %convolution_subtract_fusion.8), custom_call_target="Cholesky" | custom-call | tf_op jit(solution)/shard_map/jit(cholesky)/cholesky | solution.py:82
  525.6 6.6 while.10
  532.2 21.2 %custom-call.22 = f32[2,128,128]{1,2,0:T(8,128)} custom-call(f32[2,128,128]{2,1,0:T(8,128)} %get-tuple-element.34), custom_call_target="InvertDiagBlocksLowerTriangular" | custom-call | tf_op jit(solution)/shard_map/jit(_solve_triangular)/triangular_solve | solution.py:84
  569.4 4.4 convolution_subtract_fusion
  577.0 90.8 %collective-permute-done.3 = f32[512,1024]{1,0:T(8,128)} collective-permute-done((f32[512,1024]{1,0:T(8,128)}, f32[512,1024]{1,0:T(8,128)}, u32[]{:S(2)}, u32[]{:S(2)}) %collective-permute-start.3) | collective-permute-done | bytes 2097184 | tf_op jit(solution)/shard_map/ppermute | solution.py:14
  667.8 4.2 broadcast_select_fusion.9
  681.0 6.1 gather_fusion.14
  693.8 4.8 gather_fusion.13
  698.7 7.2 gather_fusion.15
  705.9 3.5 fusion
  713.6 11.7 %cholesky.316 = f32[128,128]{1,0:T(8,128)S(1)} custom-call(f32[128,128]{1,0:T(8,128)S(1)} %cholesky.355), custom_call_target="Cholesky" | custom-call | tf_op jit(solution)/shard_map/jit(cholesky)/cholesky | solution.py:82
  725.9 9.8 %custom-call.23 = f32[1,128,128]{1,2,0:T(8,128)S(1)} custom-call(f32[1,128,128]{2,1,0:T(8,128)S(1)} %get-tuple-element.117), custom_call_target="InvertDiagBlocksLowerTriangular" | custom-call | tf_op jit(solution)/shard_map/jit(cholesky)/cholesky | solution.py:82
  736.3 11.7 %cholesky.333 = f32[128,128]{1,0:T(8,128)S(1)} custom-call(f32[128,128]{1,0:T(8,128)S(1)} %convolution_subtract_fusion.7), custom_call_target="Cholesky" | custom-call | tf_op jit(solution)/shard_map/jit(cholesky)/cholesky | solution.py:82
  750.7 4.3 while.11
  755.0 19.7 %custom-call.24 = f32[2,128,128]{1,2,0:T(8,128)S(1)} custom-call(f32[2,128,128]{2,1,0:T(8,128)S(1)} %get-tuple-element.35), custom_call_target="InvertDiagBlocksLowerTriangular" | custom-call | tf_op jit(solution)/shard_map/jit(_solve_triangular)/triangular_solve | solution.py:84
  800.9 5.1 subtract_bitcast_fusion
  (425 shorter events, 216.7 us)
Async XLA Ops:
  7.2 22.8 %reduce-scatter.2.cloned.1.call-start = ((), (), s32[]{:S(2)}) async-start(), calls=%async_computation.1 | async-start | bytes 6291456 | tf_op jit(solution)/shard_map/reduce_scatter | solution.py:57
  15.0 191.8 %all-gather.5.cloned.1.call-start = ((), (), s32[]{:S(2)}) async-start(), calls=%async_computation.2 | async-start | bytes 1572864 | tf_op jit(solution)/shard_map/all_gather | solution.py:90
  17.7 14.8 %copy-start.46 = (s32[2,20]{1,0:T(2,128)}, s32[2,20]{1,0:T(2,128)S(1)}, u32[]{:S(2)}) copy-start(s32[2,20]{1,0:T(2,128)S(1)} %get-tuple-element.43) | copy-start | bytes 484
  17.8 14.7 %copy-start.58 = (s32[2,20]{1,0:T(2,128)}, s32[2,20]{1,0:T(2,128)S(1)}, u32[]{:S(2)}) copy-start(s32[2,20]{1,0:T(2,128)S(1)} %get-tuple-element.51) | copy-start | bytes 484
  18.5 14.0 %copy-start.52 = (s32[2,20]{1,0:T(2,128)}, s32[2,20]{1,0:T(2,128)S(1)}, u32[]{:S(2)}) copy-start(s32[2,20]{1,0:T(2,128)S(1)} %get-tuple-element.47) | copy-start | bytes 484
  19.1 13.4 %copy-start.56 = (s32[2,20]{1,0:T(2,128)}, s32[2,20]{1,0:T(2,128)S(1)}, u32[]{:S(2)}) copy-start(s32[2,20]{1,0:T(2,128)S(1)} %get-tuple-element.49) | copy-start | bytes 484
  19.9 12.7 %copy-start.50 = (s32[2,20]{1,0:T(2,128)}, s32[2,20]{1,0:T(2,128)S(1)}, u32[]{:S(2)}) copy-start(s32[2,20]{1,0:T(2,128)S(1)} %get-tuple-element.45) | copy-start | bytes 484
  30.0 48.2 %collective-permute-start = (f32[512,1024]{1,0:T(8,128)}, f32[512,1024]{1,0:T(8,128)}, u32[]{:S(2)}, u32[]{:S(2)}) collective-permute-start(f32[512,1024]{1,0:T(8,128)} %reduce-scatter.2.cloned.1.call-done), channel_id=1, source_target_pairs={{0,2},{2,0},{4,6},{6,4},{8,10},{10,8},{12,14},{14,12},{16,18},{18,... | collective-permute-start | bytes 6291464 | tf_op jit(solution)/shard_map/ppermute | solution.py:14
  161.1 40.9 %copy-start.7 = (f32[640,1280]{0,1:T(8,128)S(1)}, f32[640,1280]{0,1:T(8,128)}, u32[]{:S(2)}) copy-start(f32[640,1280]{0,1:T(8,128)} %copy-done.6) | copy-start | bytes 9830404
  169.7 21.2 %copy-start.21 = (f32[256,256]{1,0:T(8,128)}, f32[256,256]{1,0:T(8,128)S(1)}, u32[]{:S(2)}) copy-start(f32[256,256]{1,0:T(8,128)S(1)} %get-tuple-element.400) | copy-start | bytes 786436
  169.7 27.3 %copy-start.62 = (s32[2,2]{1,0:T(2,128)}, s32[2,2]{1,0:T(2,128)S(1)}, u32[]{:S(2)}) copy-start(s32[2,2]{1,0:T(2,128)S(1)} %get-tuple-element.407) | copy-start | bytes 52
  196.5 190.7 %all-gather.7.cloned.1.call-start = ((), (), s32[]{:S(2)}) async-start(), calls=%async_computation.3 | async-start | bytes 1572864 | tf_op jit(solution)/shard_map/all_gather | solution.py:90
  205.7 7.2 copy-start.59
  205.7 7.4 copy-start.61
  205.7 7.5 copy-start.60
  211.2 48.1 %collective-permute-start.1 = (f32[512,1024]{1,0:T(8,128)}, f32[512,1024]{1,0:T(8,128)}, u32[]{:S(2)}, u32[]{:S(2)}) collective-permute-start(f32[512,1024]{1,0:T(8,128)} %convolution_subtract_fusion.2), channel_id=1, source_target_pairs={{0,4},{2,6},{4,0},{6,2},{8,12},{10,14},{12,8},{14,10},{16,20},{18,... | collective-permute-start | bytes 6291464 | tf_op jit(solution)/shard_map/ppermute | solution.py:14
  290.3 7.2 copy-start.34
  290.3 7.2 copy-start.42
  290.3 7.2 copy-start.44
  301.0 43.7 %copy-start.63 = (s32[2,2]{1,0:T(2,128)S(1)}, s32[2,2]{1,0:T(2,128)}, u32[]{:S(2)}) copy-start(s32[2,2]{1,0:T(2,128)} %copy-done.62) | copy-start | bytes 52
  342.2 34.7 %copy-start.38 = (s32[2,20]{1,0:T(2,128)S(1)}, s32[2,20]{1,0:T(2,128)}, u32[]{:S(2)}) copy-start(s32[2,20]{1,0:T(2,128)} %get-tuple-element.46) | copy-start | bytes 484
  342.2 34.7 %copy-start.39 = (s32[2,20]{1,0:T(2,128)S(1)}, s32[2,20]{1,0:T(2,128)}, u32[]{:S(2)}) copy-start(s32[2,20]{1,0:T(2,128)} %get-tuple-element.48) | copy-start | bytes 484
  342.2 40.0 %copy-start.57 = (s32[2,20]{1,0:T(2,128)S(1)}, s32[2,20]{1,0:T(2,128)}, u32[]{:S(2)}) copy-start(s32[2,20]{1,0:T(2,128)} %copy-done.56) | copy-start | bytes 484
  342.2 40.1 %copy-start.9 = (f32[640,1280]{0,1:T(8,128)S(1)}, f32[640,1280]{0,1:T(8,128)}, u32[]{:S(2)}) copy-start(f32[640,1280]{0,1:T(8,128)} %copy-done.8) | copy-start | bytes 9830404
  350.1 21.1 %copy-start.22 = (f32[256,256]{1,0:T(8,128)}, f32[256,256]{1,0:T(8,128)S(1)}, u32[]{:S(2)}) copy-start(f32[256,256]{1,0:T(8,128)S(1)} %get-tuple-element.401) | copy-start | bytes 786436
  376.8 192.5 %all-gather.9.cloned.1.call-start = ((), (), s32[]{:S(2)}) async-start(), calls=%async_computation.4 | async-start | bytes 1572864 | tf_op jit(solution)/shard_map/all_gather | solution.py:90
  386.1 7.3 copy-start.53
  386.1 7.5 copy-start.55
  386.1 7.6 copy-start.54
  391.6 48.2 %collective-permute-start.2 = (f32[512,1024]{1,0:T(8,128)}, f32[512,1024]{1,0:T(8,128)}, u32[]{:S(2)}, u32[]{:S(2)}) collective-permute-start(f32[512,1024]{1,0:T(8,128)} %convolution_subtract_fusion.1), channel_id=1, source_target_pairs={{0,8},{2,10},{4,12},{6,14},{8,0},{10,2},{12,4},{14,6},{16,24},{18,... | collective-permute-start | bytes 6291464 | tf_op jit(solution)/shard_map/ppermute | solution.py:14
  470.7 7.2 copy-start.43
  470.7 7.2 copy-start.45
  523.1 36.0 %copy-start.36 = (s32[2,20]{1,0:T(2,128)S(1)}, s32[2,20]{1,0:T(2,128)}, u32[]{:S(2)}) copy-start(s32[2,20]{1,0:T(2,128)} %get-tuple-element.42) | copy-start | bytes 484
  523.1 36.0 %copy-start.37 = (s32[2,20]{1,0:T(2,128)S(1)}, s32[2,20]{1,0:T(2,128)}, u32[]{:S(2)}) copy-start(s32[2,20]{1,0:T(2,128)} %get-tuple-element.44) | copy-start | bytes 484
  523.1 41.1 %copy-start.51 = (s32[2,20]{1,0:T(2,128)S(1)}, s32[2,20]{1,0:T(2,128)}, u32[]{:S(2)}) copy-start(s32[2,20]{1,0:T(2,128)} %copy-done.50) | copy-start | bytes 484
  523.1 41.3 %copy-start.5 = (f32[640,1280]{0,1:T(8,128)S(1)}, f32[640,1280]{0,1:T(8,128)}, u32[]{:S(2)}) copy-start(f32[640,1280]{0,1:T(8,128)} %copy-done.4) | copy-start | bytes 9830404
  532.2 21.2 %copy-start.23 = (f32[256,256]{1,0:T(8,128)}, f32[256,256]{1,0:T(8,128)S(1)}, u32[]{:S(2)}) copy-start(f32[256,256]{1,0:T(8,128)S(1)} %get-tuple-element.402) | copy-start | bytes 786436
  559.0 241.9 %all-gather.11.cloned.1.call-start = ((), (), s32[]{:S(2)}) async-start(), calls=%async_computation.5 | async-start | bytes 1572864 | tf_op jit(solution)/shard_map/all_gather | solution.py:90
  568.1 8.3 %copy-start.47 = (s32[2,20]{1,0:T(2,128)S(1)}, s32[2,20]{1,0:T(2,128)}, u32[]{:S(2)}) copy-start(s32[2,20]{1,0:T(2,128)} %copy-done.46) | copy-start | bytes 484
  568.1 8.5 %copy-start.49 = (s32[2,20]{1,0:T(2,128)S(1)}, s32[2,20]{1,0:T(2,128)}, u32[]{:S(2)}) copy-start(s32[2,20]{1,0:T(2,128)} %get-tuple-element.142) | copy-start | bytes 484
  568.1 8.6 %copy-start.48 = (s32[2,20]{1,0:T(2,128)S(1)}, s32[2,20]{1,0:T(2,128)}, u32[]{:S(2)}) copy-start(s32[2,20]{1,0:T(2,128)} %get-tuple-element.148) | copy-start | bytes 484
  573.8 94.0 %collective-permute-start.3 = (f32[512,1024]{1,0:T(8,128)}, f32[512,1024]{1,0:T(8,128)}, u32[]{:S(2)}, u32[]{:S(2)}) collective-permute-start(f32[512,1024]{1,0:T(8,128)} %convolution_subtract_fusion), channel_id=1, source_target_pairs={{0,16},{2,18},{4,20},{6,22},{8,24},{10,26},{12,28},{14,30},{16,0},... | collective-permute-start | bytes 6291464 | tf_op jit(solution)/shard_map/ppermute | solution.py:14
  698.7 7.2 copy-start.31
  698.7 7.2 copy-start.40
  698.7 7.2 copy-start.41
  709.4 41.3 %copy-start.64 = (s32[2,2]{1,0:T(2,128)S(1)}, s32[2,2]{1,0:T(2,128)}, u32[]{:S(2)}) copy-start(s32[2,2]{1,0:T(2,128)} %get-tuple-element.409) | copy-start | bytes 52
  750.0 27.5 %copy-start.27 = (f32[256,256]{1,0:T(8,128)S(1)}, f32[256,256]{1,0:T(8,128)}, u32[]{:S(2)}) copy-start(f32[256,256]{1,0:T(8,128)} %get-tuple-element.97) | copy-start | bytes 786436
  778.2 14.2 %copy-start.11 = (f32[640,1280]{0,1:T(8,128)S(1)}, f32[640,1280]{0,1:T(8,128)}, u32[]{:S(2)}) copy-start(f32[640,1280]{0,1:T(8,128)} %copy-done.10) | copy-start | bytes 9830404
  (26 other events, 92.4 us)
Sparse Core Ops, SparseCore 0:
  15.1 14.7 reduce-scatter.1
  196.6 10.1 all-gather.4
  377.0 10.2 all-gather.6
  559.1 10.1 all-gather.8
  777.6 10.1 all-gather.10
where the time goes:
time: 822 us; the launch traced here: 813 us
  other arithmetic  307 us (37%)
  waiting for transfers between devices  241 us (29%)
  local copies, waits for them, and re-layouts  186 us (23%)
  matrix products  40.3 us (5%)
  between operations  20.6 us (3%)
  blocking collectives  8.94 us (1%)
    ppermute x4, waiting for transfers between devices, swapped(): return lax.ppermute(value, axis, pairs)  227 us
    another operation x28, other arithmetic, body(): lower_factor = jnp.linalg.cholesky(pivot_block)  138 us
    another operation x9, other arithmetic, body(): jax.scipy.linalg.solve_triangular(lower_factor, coupling.T, lower=True)  89.9 us
    gather x8, local copies, waits for them, and re-layouts, place_child(): jnp.take(jnp.take(child, row_source, axis=0), column_source, axis=1)  48 us
    gather x8, local copies, waits for them, and re-layouts, place_child(): jnp.take(child, row_source, axis=0)  38 us
    select_n x12, other arithmetic, place_child(): jnp.take(child, row_source, axis=0)  27.8 us
    another operation x29, local copies, waits for them, and re-layouts, body(): jax.scipy.linalg.solve_triangular(lower_factor, coupling.T, lower=True)  23.2 us
    select_n x8, local copies, waits for them, and re-layouts, place_child(): jnp.take(child, row_source, axis=0)  21.7 us
  transfers between devices with their start and end apart: 9, of which 8 were waited for; matrix products, arithmetic and copies ran while one was open for 7% of the time, Pallas kernels for 0%

commit v1 on v0

v1 whole, which is shorter than its diff:
```python
import functools

import jax
import jax.numpy as jnp
from jax import lax
from jax.experimental import pallas as pl
from jax.experimental.pallas import tpu as pltpu
from jax.sharding import PartitionSpec as P

KP = 256
SB = 32
LEVELS = 4
T = 128
NB = 32
ROUND = 4
MESH = pl.DeviceIdType.MESH
F32 = jnp.float32
BF16 = jnp.bfloat16
VMEM_BYTES = 56 * 2**20


def split2(x):
    hi = x.astype(BF16)
    return hi, (x - hi.astype(F32)).astype(BF16)


def dot3(a, b, dims):
    (ah, al), (bh, bl) = a, b
    one = functools.partial(
        lax.dot_general, dimension_numbers=(dims, ((), ())), preferred_element_type=F32
    )
    return one(ah, bh) + (one(ah, bl) + one(al, bh))


def exact_dot(a, b, dims):
    return lax.dot_general(
        a, b, (dims, ((), ())), precision=lax.Precision.HIGHEST, preferred_element_type=F32
    )


def mirror_strip(ref, i):
    for k in range(i):
        ref[k * T : (k + 1) * T, i * T : (i + 1) * T] = ref[
            i * T : (i + 1) * T, k * T : (k + 1) * T
        ].T


def strip_of(ref, i):
    return ref.at[pl.ds(i * T, T), pl.ds(0, (i + 1) * T)]


def gram_kernel(strips, m_ref, out_ref, got, send_sem, recv_sem):
    leaf, col = lax.axis_index("leaf"), lax.axis_index("col")
    barrier = pltpu.get_barrier_semaphore()
    pl.semaphore_signal(barrier, inc=1, device_id=(leaf, 1 - col), device_id_type=MESH)
    part = got.at[0]
    land = got.at[1]
    copies = []
    for n, i in enumerate(reversed(range(strips))):
        part[i * T : (i + 1) * T, : (i + 1) * T] = lax.dot_general(
            m_ref[:, i * T : (i + 1) * T],
            m_ref[:, : (i + 1) * T],
            (((0,), (0,)), ((), ())),
            preferred_element_type=F32,
        )
        if n == 0:
            pl.semaphore_wait(barrier, 1)
        copy = pltpu.make_async_remote_copy(
            src_ref=strip_of(part, i),
            dst_ref=strip_of(land, i),
            send_sem=send_sem.at[i],
            recv_sem=recv_sem.at[i],
            device_id=(leaf, 1 - col),
            device_id_type=MESH,
        )
        copy.start()
        copies.append((i, copy))
    for i, copy in copies:
        copy.wait_recv()
        rows, cols = slice(i * T, (i + 1) * T), slice(0, (i + 1) * T)
        out_ref[rows, cols] = part[rows, cols] + land[rows, cols]
        mirror_strip(out_ref, i)
    for _, copy in copies:
        copy.wait_send()


def gram(masked, collective):
    width = masked.shape[1]
    strips = width // T
    return pl.pallas_call(
        functools.partial(gram_kernel, strips),
        out_shape=jax.ShapeDtypeStruct((width, width), F32),
        in_specs=[pl.BlockSpec(memory_space=pltpu.VMEM)],
        out_specs=pl.BlockSpec(memory_space=pltpu.VMEM),
        scratch_shapes=[
            pltpu.VMEM((2, width, width), F32),
            pltpu.SemaphoreType.DMA((strips,)),
            pltpu.SemaphoreType.DMA((strips,)),
        ],
        compiler_params=pltpu.CompilerParams(
            collective_id=collective, has_side_effects=True, vmem_limit_bytes=VMEM_BYTES
        ),
        name="gram",
    )(masked)


def exchange_kernel(strips, level, c_ref, out_ref, land, send_sem, recv_sem, fsend_sem, frecv_sem):
    leaf, col = lax.axis_index("leaf"), lax.axis_index("col")
    stride = 2**level
    bit = (leaf // stride) % 2
    partner = leaf + stride - 2 * stride * bit
    barrier = pltpu.get_barrier_semaphore()
    pl.semaphore_signal(barrier, inc=1, device_id=(partner, col), device_id_type=MESH)
    pl.semaphore_signal(barrier, inc=1, device_id=(leaf, 1 - col), device_id_type=MESH)
    pl.semaphore_wait(barrier, 2)
    orders = [
        [i for i in reversed(range(strips)) if (i % 4 in (0, 3)) == (core == 0)]
        for core in range(2)
    ]

    for core in range(2):

        @pl.when(col == core)
        def _():
            sends, forwards = [], []
            for i in orders[core]:
                copy = pltpu.make_async_remote_copy(
                    src_ref=strip_of(c_ref, i),
                    dst_ref=strip_of(land, i),
                    send_sem=send_sem.at[i],
                    recv_sem=recv_sem.at[i],
                    device_id=(partner, col),
                    device_id_type=MESH,
                )
                copy.start()
                sends.append(copy)
            theirs = []
            for i in orders[1 - core]:
                theirs.append(
                    pltpu.make_async_remote_copy(
                        src_ref=strip_of(land, i),
                        dst_ref=strip_of(land, i),
                        send_sem=fsend_sem.at[i],
                        recv_sem=frecv_sem.at[i],
                        device_id=(leaf, 1 - col),
                        device_id_type=MESH,
                    )
                )
            for n, i in enumerate(orders[core]):
                sends[n].wait_recv()
                forward = pltpu.make_async_remote_copy(
                    src_ref=strip_of(land, i),
                    dst_ref=strip_of(land, i),
                    send_sem=fsend_sem.at[i],
                    recv_sem=frecv_sem.at[i],
                    device_id=(leaf, 1 - col),
                    device_id_type=MESH,
                )
                forward.start()
                forwards.append(forward)
                out_ref[i * T : (i + 1) * T, : (i + 1) * T] = land[
                    i * T : (i + 1) * T, : (i + 1) * T
                ]
                mirror_strip(out_ref, i)
                if n:
                    j = orders[1 - core][n - 1]
                    theirs[n - 1].wait_recv()
                    out_ref[j * T : (j + 1) * T, : (j + 1) * T] = land[
                        j * T : (j + 1) * T, : (j + 1) * T
                    ]
                    mirror_strip(out_ref, j)
            j = orders[1 - core][-1]
            theirs[-1].wait_recv()
            out_ref[j * T : (j + 1) * T, : (j + 1) * T] = land[
                j * T : (j + 1) * T, : (j + 1) * T
            ]
            mirror_strip(out_ref, j)
            for copy in sends + forwards:
                copy.wait_send()


def exchange(current, level, collective):
    width = current.shape[0]
    strips = width // T
    return pl.pallas_call(
        functools.partial(exchange_kernel, strips, level),
        out_shape=jax.ShapeDtypeStruct((width, width), F32),
        in_specs=[pl.BlockSpec(memory_space=pltpu.VMEM)],
        out_specs=pl.BlockSpec(memory_space=pltpu.VMEM),
        scratch_shapes=[pltpu.VMEM((width, width), F32)]
        + [pltpu.SemaphoreType.DMA((strips,)) for _ in range(4)],
        compiler_params=pltpu.CompilerParams(
            collective_id=collective, has_side_effects=True, vmem_limit_bytes=VMEM_BYTES
        ),
        name="exchange",
    )(current)


def factor_small(diag):
    row = lax.broadcasted_iota(jnp.int32, (NB, T), 0)
    lane = lax.broadcasted_iota(jnp.int32, (NB, T), 1)
    m = jnp.where(lane < NB, diag, jnp.where(lane == row + NB, 1.0, 0.0))
    for j in range(0, NB, ROUND):
        cols = [jnp.broadcast_to(m[:, j + q : j + q + 1], (NB, T)) for q in range(ROUND)]
        rows = [m[j + p : j + p + 1, :] for p in range(ROUND)]
        b = [[cols[q][j + p : j + p + 1, :] for q in range(ROUND)] for p in range(ROUND)]
        update = m
        for q in range(ROUND):
            r = 1.0 / b[q][q]
            factor = cols[q] * r
            update = update - factor * rows[q]
            for t in range(q + 1, ROUND):
                cols[t] = cols[t] - factor * b[q][t]
            for p in range(q + 1, ROUND):
                g = b[p][q] * r
                rows[p] = rows[p] - g * rows[q]
                for t in range(q + 1, ROUND):
                    b[p][t] = b[p][t] - g * b[q][t]
        m_next = jnp.where(row >= j + ROUND, update, m)
        for p in range(1, ROUND):
            m_next = jnp.where(row == j + p, rows[p], m_next)
        m = m_next
    pivots = jnp.sum(jnp.where(lane == row, m, 0.0), axis=1, keepdims=True)
    inverse = pltpu.roll(m, T - NB, 1) * lax.rsqrt(pivots)
    return inverse[:, :NB]


def front_kernel(
    strips, last, idx_ref, own_ref, other_ref, factor_ref, next_ref, front, work, upper, low, u, uh, ul
):
    subs = front.shape[0] // SB
    per = T // SB
    pivot_tiles = KP // T
    tiles = front.shape[1] // T
    lane_group = lax.broadcasted_iota(jnp.int32, (SB, T), 1) // SB

    def entry(child, field, s):
        return idx_ref[(child * 5 + field) * subs + s]

    def assemble(r, tile_count):
        base = pl.multiple_of(r * SB, SB)
        for child, ref in ((0, own_ref), (1, other_ref)):
            present = entry(child, 1, r) > 0

            @pl.when(present)
            def _():
                start = pl.multiple_of(entry(child, 0, r) * SB, SB)
                for t in range(tile_count):
                    if child:
                        total = front[pl.ds(base, SB), t * T : (t + 1) * T]
                    else:
                        total = jnp.zeros((SB, T), F32)
                    for q in range(per):
                        s = t * per + q
                        tile = ref[
                            pl.ds(start, SB),
                            pl.ds(pl.multiple_of(entry(child, 2, s) * T, T), T),
                        ]
                        moved = pltpu.roll(tile, entry(child, 3, s), 1)
                        picked = jnp.where(lane_group == entry(child, 4, s), moved, 0.0)
                        total = total + picked
                    front[pl.ds(base, SB), t * T : (t + 1) * T] = total

            if not child:

                @pl.when(jnp.logical_not(present))
                def _():
                    front[pl.ds(base, SB), : tile_count * T] = jnp.zeros(
                        (SB, tile_count * T), F32
                    )

    @pl.loop(0, KP // SB)
    def _(r):
        assemble(r, pivot_tiles)

    @pl.loop(KP // SB, subs)
    def _(r):
        assemble(r, tiles)

    work[...] = front[:KP, :KP]
    lanes = lax.broadcasted_iota(jnp.int32, (NB, KP), 1)
    rows32 = lax.broadcasted_iota(jnp.int32, (NB, KP), 0)
    for b in range(KP // NB):
        lo = b * NB
        panel = work[lo : lo + NB, :]
        tile = lo // T
        diag = panel[:, tile * T : (tile + 1) * T]
        if lo % T:
            diag = pltpu.roll(diag, T - lo % T, 1)
        w = factor_small(diag)
        in_diag = (lanes >= lo) & (lanes < lo + NB)
        opened = jnp.where(in_diag, jnp.where(lanes == rows32 + lo, 1.0, 0.0), panel)
        q = exact_dot(w, opened, ((1,), (0,)))
        r_diag = exact_dot(w, jnp.where(in_diag, panel, 0.0), ((1,), (0,)))
        upper[lo : lo + NB, :] = jnp.where(
            lanes < lo + NB, jnp.where(lanes >= rows32 + lo, r_diag, 0.0), q
        )
        low[lo : lo + NB, :] = jnp.where(lanes <= rows32 + lo, q, 0.0)
        if lo + NB < KP:
            below = lo + NB
            right = jnp.where(lanes >= below, q, 0.0)
            change = exact_dot(right, q, ((0,), (0,)))
            lanes_b = lax.broadcasted_iota(jnp.int32, (KP - below, KP), 1)
            rest = work[below:, :]
            rest = jnp.where((lanes_b >= lo) & (lanes_b < below), 0.0, rest)
            work[below:, :] = rest - change[below:, :]

    col = lax.axis_index("col")
    share = KP // 2
    work[...] = upper[...].T
    factor_ref[:share, :] = work[pl.ds(pl.multiple_of(col * share, share), share), :]
    inverse = split2(low[...])

    @pl.loop(0, strips)
    def _(i):
        base = pl.multiple_of(i * T, T)
        coupling = front[pl.ds(pl.multiple_of(KP + base, T), T), :KP]
        strip = dot3(split2(coupling), inverse, ((1,), (1,)))
        u[pl.ds(base, T), :] = strip
        hi, lo = split2(strip)
        uh[pl.ds(base, T), :] = hi
        ul[pl.ds(base, T), :] = lo

    half = strips * T // 2
    factor_ref[share:, :] = u[pl.ds(pl.multiple_of(col * half, half), half), :]
    offset = col * half if last else 0
    whole = (uh[...], ul[...])

    @pl.loop(0, strips // 2 if last else strips)
    def _(i):
        base = pl.multiple_of(i * T, T)
        at = pl.multiple_of(base + offset, T)
        product = dot3((uh[pl.ds(at, T), :], ul[pl.ds(at, T), :]), whole, ((1,), (1,)))
        next_ref[pl.ds(base, T), :] = front[pl.ds(pl.multiple_of(at + KP, T), T), KP:] - product


def merge(own, other, index, last):
    width = own.shape[0]
    front_width = width + KP
    out_rows = width // 2 if last else width
    vmem = pl.BlockSpec(memory_space=pltpu.VMEM)
    return pl.pallas_call(
        functools.partial(front_kernel, width // T, last),
        out_shape=(
            jax.ShapeDtypeStruct((front_width // 2, KP), F32),
            jax.ShapeDtypeStruct((out_rows, width), F32),
        ),
        in_specs=[pl.BlockSpec(memory_space=pltpu.SMEM), vmem, vmem],
        out_specs=(vmem, vmem),
        scratch_shapes=[
            pltpu.VMEM((front_width, front_width), F32),
            pltpu.VMEM((KP, KP), F32),
            pltpu.VMEM((KP, KP), F32),
            pltpu.VMEM((KP, KP), F32),
            pltpu.VMEM((width, KP), F32),
            pltpu.VMEM((width, KP), BF16),
            pltpu.VMEM((width, KP), BF16),
        ],
        compiler_params=pltpu.CompilerParams(vmem_limit_bytes=VMEM_BYTES),
        name="front",
    )(index, own, other)


def index_table(child_maps, sub_count):
    col_count, child_subs = child_maps.shape
    per = T // SB
    pivot_subs = KP // col_count // SB
    matches = (child_maps[:, :, None] == lax.iota(jnp.int32, sub_count)[None, None, :]).astype(
        jnp.int32
    )
    offset = lax.iota(jnp.int32, col_count)[:, None] * child_subs
    source = jnp.sum(matches * lax.iota(jnp.int32, child_subs)[None, :, None], axis=1) + offset
    present = jnp.sum(matches, axis=1)

    def pivots_first(table):
        return jnp.concatenate(
            [table[:, :pivot_subs].reshape(-1), table[:, pivot_subs:].reshape(-1)]
        )

    source, present = pivots_first(source), pivots_first(present)
    place = lax.iota(jnp.int32, source.shape[0]) % per
    shift = (place - source % per + per) % per * SB
    group = jnp.where(present > 0, place, -1)
    return jnp.concatenate([source, present, source // per, shift, group])


def body(rows_a, stair_counts, block_maps):
    col_count = lax.axis_size("col")
    col_index = lax.axis_index("col")
    leaf_index = lax.axis_index("leaf")
    local_rows, width = rows_a.shape
    front_cols = (width + KP) // col_count
    sub_count = front_cols // SB
    bounds = jnp.cumsum(stair_counts[0])
    row_index = col_index * local_rows + lax.iota(jnp.int32, local_rows)
    leading = jnp.sum((bounds[None, :] <= row_index[:, None]).astype(jnp.int32), axis=1)
    column_block = lax.iota(jnp.int32, width) // (width // stair_counts.shape[1])
    masked = jnp.where(column_block[None, :] >= leading[:, None], rows_a, jnp.zeros_like(rows_a))
    current = gram(masked, 0)
    factors = []
    for level in range(LEVELS):
        other = exchange(current, level, level + 1)
        pair_bit = leaf_index >> level & 1
        front_maps = lax.dynamic_index_in_dim(
            block_maps[level], leaf_index >> level + 1, 0, keepdims=False
        )
        own_maps = lax.dynamic_index_in_dim(front_maps, pair_bit, 0, keepdims=False)
        other_maps = lax.dynamic_index_in_dim(front_maps, 1 - pair_bit, 0, keepdims=False)
        index = jnp.concatenate(
            [index_table(own_maps, sub_count), index_table(other_maps, sub_count)]
        )
        factor, current = merge(current, other, index, level == LEVELS - 1)
        factors.append(factor)
    return (jnp.stack(factors)[:, None], current[None])


def solution(mesh):
    return jax.shard_map(
        body,
        mesh=mesh,
        in_specs=(P(("leaf", "col"), None), P("leaf", None), P()),
        out_specs=(P(None, "leaf", "col", None), P("leaf", "col", None)),
        check_vma=False,
    )
```

time: 822 us -> 359 us (0.44)
  Pallas kernels: 0 us -> 335 us
  other arithmetic: 307 us -> 9.98 us
  waiting for transfers between devices: 241 us -> 0 us
  local copies, waits for them, and re-layouts: 186 us -> 7.26 us
  matrix products: 40.3 us -> 0 us
  between operations: 20.6 us -> 1.08 us
  blocking collectives: 8.94 us -> 0 us
    pallas_call x0 -> x9, Pallas kernels: none -> 335 us  [the longest x4 163 us: merge(): pl.pallas_call(functools.partial(front_kernel, width // T, last), out_sha...]
    another operation x42 -> x1, other arithmetic: 235 us -> 0.83 us  [the longest x28 138 us: body(): lower_factor = jnp.linalg.cholesky(pivot_block)]
    ppermute x4 -> x0, waiting for transfers between devices: 227 us -> none  [swapped(): return lax.ppermute(value, axis, pairs)]
    gather x16 -> x0, local copies, waits for them, and re-layouts: 86 us -> none  [the longest x8 48 us: place_child(): jnp.take(jnp.take(child, row_source, axis=0), column_source, axis=1)]
    select_n x20 -> x17, other arithmetic: 44.5 us -> 4.73 us  [the longest x1 3.45 us: body(): jnp.where(column_block[None, :] >= leading[:, None], rows_a, jnp.zeros_li...]
    dot_general x5 -> x0, matrix products: 25.1 us -> none  [the longest x4 18.3 us: body(): lax.dot_general(upper_rows, lax.all_gather(upper_rows, 'col', axis=0, til...]
    another operation x37 -> x0, local copies, waits for them, and re-layouts: 23.3 us -> none  [the longest x29 23.2 us: body(): jax.scipy.linalg.solve_triangular(lower_factor, coupling.T, lower=True)]
    select_n x8 -> x0, local copies, waits for them, and re-layouts: 21.7 us -> none  [place_child(): jnp.take(child, row_source, axis=0)]
  transfers between devices with their start and end apart: 9 -> 0, of which waited for: 8 -> 0; matrix products, arithmetic and copies ran while one was open for 7% -> 0% of each run, Pallas kernels for 0% -> 0%
where the time goes in v1:
time: 359 us; the launch traced here: 353 us
  Pallas kernels  335 us (93%)
  other arithmetic  9.98 us (3%)
  local copies, waits for them, and re-layouts  7.26 us (2%)
    pallas_call x4, Pallas kernels, merge(): pl.pallas_call(functools.partial(front_kernel, width // T, last), out_sha...  163 us
    pallas_call x4, Pallas kernels, exchange(): pl.pallas_call(functools.partial(exchange_kernel, strips, level), out_sha...  163 us
    pallas_call x1, Pallas kernels, gram(): pl.pallas_call(functools.partial(gram_kernel, strips), out_shape=jax.Shap...  8.65 us

profile of v1, /device:TPU:0, one launch (start us, length us, event | category | flops | bytes accessed | tf_op | source)
XLA Modules:
  0.0 353.2 jit_solution(8501577667089820491)
XLA Ops:
  0.7 0.8 reduce-window.8
  1.6 0.8 fusion.35
  2.4 0.1 convert_reduce_fusion.3
  2.5 0.1 reshape.211
  2.7 0.1 reshape.212
  2.8 0.1 convert_reduce_fusion.7
  2.9 0.1 reshape.193
  3.1 0.1 reshape.194
  3.2 0.1 convert_reduce_fusion.4
  3.3 0.1 reshape.207
  3.5 0.1 reshape.208
  3.7 0.1 convert_reduce_fusion.2
  3.7 0.1 reshape.215
  3.9 0.1 reshape.216
  4.1 0.1 convert_reduce_fusion.1
  4.5 0.1 convert_reduce_fusion.8
  4.6 0.1 reshape.189
  4.7 0.1 reshape.190
  4.9 0.1 convert_reduce_fusion.6
  5.3 0.1 convert_reduce_fusion.5
  6.3 0.1 reshape.192
  7.0 0.1 reshape.214
  7.2 0.1 reshape.218
  7.4 0.1 reshape.188
  7.5 0.1 reshape.204
  7.7 0.1 fusion.19
  7.9 0.1 fusion.26
  8.0 0.1 fusion.25
  8.2 0.7 concatenate.83.idx_ref
  8.9 0.1 fusion.24
  9.1 0.1 fusion.23
  9.2 0.7 concatenate.78.idx_ref
  9.9 0.1 fusion.22
  10.1 0.1 fusion.21
  10.2 0.7 concatenate.73.idx_ref
  10.9 0.1 fusion.20
  11.1 0.6 concatenate.68.idx_ref
  11.7 3.5 compare_select_fusion.m_ref
  15.2 8.7 %gram.1.c_ref.own_ref = f32[1024,1024]{1,0:T(8,128)} custom-call(bf16[1024,1024]{1,0:T(8,128)(2,1)} %compare_select_fusion.m_ref), custom_call_target="tpu_custom_call" | custom-call | tf_op jit(solution)/shard_map/gram/pallas_call | solution.py:90
  23.8 35.1 %exchange.4.other_ref = f32[1024,1024]{1,0:T(8,128)} custom-call(f32[1024,1024]{1,0:T(8,128)} %gram.1.c_ref.own_ref), custom_call_target="tpu_custom_call" | custom-call | tf_op jit(solution)/shard_map/exchange/pallas_call | solution.py:185
  58.9 41.5 %front.4 = (f32[640,256]{1,0:T(8,128)}, f32[1024,1024]{1,0:T(8,128)}) custom-call(s32[400]{0:T(512)} %concatenate.68.idx_ref, f32[1024,1024]{1,0:T(8,128)} %gram.1.c_ref.own_ref, f32[1024,1024]{1,0:T(8,128)} %exchange.4.other_ref), custom_call_target="tpu_custom_call" | custom-call | tf_op jit(solution)/shard_map/front/pallas_call | solution.py:342
  100.4 33.8 %exchange.5.other_ref = f32[1024,1024]{1,0:T(8,128)} custom-call(f32[1024,1024]{1,0:T(8,128)} %get-tuple-element.11.c_ref.own_ref), custom_call_target="tpu_custom_call" | custom-call | tf_op jit(solution)/shard_map/exchange/pallas_call | solution.py:185
  134.3 42.0 %front.5 = (f32[640,256]{1,0:T(8,128)}, f32[1024,1024]{1,0:T(8,128)}) custom-call(s32[400]{0:T(512)} %concatenate.73.idx_ref, f32[1024,1024]{1,0:T(8,128)} %get-tuple-element.11.c_ref.own_ref, f32[1024,1024]{1,0:T(8,128)} %exchange.5.other_ref), custom_call_target="tpu_custom_call" | custom-call | tf_op jit(solution)/shard_map/front/pallas_call | solution.py:342
  176.3 33.8 %exchange.6.other_ref = f32[1024,1024]{1,0:T(8,128)} custom-call(f32[1024,1024]{1,0:T(8,128)} %get-tuple-element.13.c_ref.own_ref), custom_call_target="tpu_custom_call" | custom-call | tf_op jit(solution)/shard_map/exchange/pallas_call | solution.py:185
  210.1 41.4 %front.6 = (f32[640,256]{1,0:T(8,128)}, f32[1024,1024]{1,0:T(8,128)}) custom-call(s32[400]{0:T(512)} %concatenate.78.idx_ref, f32[1024,1024]{1,0:T(8,128)} %get-tuple-element.13.c_ref.own_ref, f32[1024,1024]{1,0:T(8,128)} %exchange.6.other_ref), custom_call_target="tpu_custom_call" | custom-call | tf_op jit(solution)/shard_map/front/pallas_call | solution.py:342
  251.5 60.0 %exchange.7.other_ref = f32[1024,1024]{1,0:T(8,128)} custom-call(f32[1024,1024]{1,0:T(8,128)} %get-tuple-element.15.c_ref.own_ref), custom_call_target="tpu_custom_call" | custom-call | tf_op jit(solution)/shard_map/exchange/pallas_call | solution.py:185
  311.6 38.5 %front.7 = (f32[640,256]{1,0:T(8,128)}, f32[512,1024]{1,0:T(8,128)}) custom-call(s32[400]{0:T(512)} %concatenate.83.idx_ref, f32[1024,1024]{1,0:T(8,128)} %get-tuple-element.15.c_ref.own_ref, f32[1024,1024]{1,0:T(8,128)} %exchange.7.other_ref), custom_call_target="tpu_custom_call" | custom-call | tf_op jit(solution)/shard_map/front/pallas_call | solution.py:342
  350.1 2.8 maximum_bitcast_fusion
  (62 shorter events, 4.0 us)
Async XLA Ops:
  311.5 38.5 %copy-start = (f32[640,256]{1,0:T(8,128)S(1)}, f32[640,256]{1,0:T(8,128)}, u32[]{:S(2)}) copy-start(f32[640,256]{1,0:T(8,128)} %get-tuple-element.10) | copy-start | bytes 1966084
  311.6 38.5 %copy-start.1 = (f32[640,256]{1,0:T(8,128)S(1)}, f32[640,256]{1,0:T(8,128)}, u32[]{:S(2)}) copy-start(f32[640,256]{1,0:T(8,128)} %get-tuple-element.12) | copy-start | bytes 1966084
  311.6 38.5 %copy-start.2 = (f32[640,256]{1,0:T(8,128)S(1)}, f32[640,256]{1,0:T(8,128)}, u32[]{:S(2)}) copy-start(f32[640,256]{1,0:T(8,128)} %get-tuple-element.14) | copy-start | bytes 1966084

commit v2 on v1

--- a/solution.py
+++ b/solution.py
@@ -11,6 +11,7 @@
 SB = 32
 LEVELS = 4
 T = 128
+G = 256
 NB = 32
 ROUND = 4
 MESH = pl.DeviceIdType.MESH
@@ -104,79 +105,157 @@
     )(masked)
 
 
-def exchange_kernel(strips, level, c_ref, out_ref, land, send_sem, recv_sem, fsend_sem, frecv_sem):
+def pieces_of(quarter, strips):
+    cut = []
+    for k in range(quarter, strips // 2, 4):
+        for i in (strips - 1 - k, k):
+            for at in range(0, i + 1, 2):
+                cut.append((i, at, min(2, i + 1 - at)))
+    return cut
+
+
+def exchange_kernel(strips, level, c_ref, out_ref, send_sem, recv_sem):
     leaf, col = lax.axis_index("leaf"), lax.axis_index("col")
+    side = leaf % 2
     stride = 2**level
     bit = (leaf // stride) % 2
-    partner = leaf + stride - 2 * stride * bit
+    relay = level == LEVELS - 1
+    split = level > 0
+    cuts = [pieces_of(quarter, strips) for quarter in range(4)]
+    count = len(cuts[0])
+    beside = (leaf + 1 - 2 * side, col)
+    sibling = (leaf, 1 - col)
+    if relay:
+        near = stride // 2
+        near_bit = (leaf // near) % 2
+        inner = bit + near_bit == 1
+        partner = (leaf + near - 2 * near * bit, col)
+        outer = (leaf + near - 2 * near * near_bit, col)
+    else:
+        partner = (leaf + stride - 2 * stride * bit, col)
+
     barrier = pltpu.get_barrier_semaphore()
-    pl.semaphore_signal(barrier, inc=1, device_id=(partner, col), device_id_type=MESH)
-    pl.semaphore_signal(barrier, inc=1, device_id=(leaf, 1 - col), device_id_type=MESH)
-    pl.semaphore_wait(barrier, 2)
-    orders = [
-        [i for i in reversed(range(strips)) if (i % 4 in (0, 3)) == (core == 0)]
-        for core in range(2)
-    ]
+
+    def greet(device):
+        pl.semaphore_signal(barrier, inc=1, device_id=device, device_id_type=MESH)
+
+    greet(sibling)
+    if split:
+        greet(beside)
+    if relay:
+        greet(outer)
+
+        @pl.when(inner)
+        def _():
+            greet(partner)
+            pl.semaphore_wait(barrier, 4)
+
+        @pl.when(jnp.logical_not(inner))
+        def _():
+            pl.semaphore_wait(barrier, 3)
+
+    else:
+        greet(partner)
+        pl.semaphore_wait(barrier, 3 if split else 2)
+
+    def copy_of(kind, quarter, n, source, device):
+        i, at, blocks = cuts[quarter][n]
+        place = (pl.ds(i * T, T), pl.ds(at * T, blocks * T))
+        return pltpu.make_async_remote_copy(
+            src_ref=source.at[place],
+            dst_ref=out_ref.at[place],
+            send_sem=send_sem.at[kind, quarter, n],
+            recv_sem=recv_sem.at[quarter, n],
+            device_id=device,
+            device_id_type=MESH,
+        )
+
+    def mirror(quarter, n):
+        i, at, blocks = cuts[quarter][n]
+        for k in range(at, min(at + blocks, i)):
+            out_ref[k * T : (k + 1) * T, i * T : (i + 1) * T] = out_ref[
+                i * T : (i + 1) * T, k * T : (k + 1) * T
+            ].T
+
+    def cross(quarter, n):
+        return copy_of(0, quarter, n, c_ref, partner)
+
+    def to_sibling(quarter, n):
+        return copy_of(1, quarter, n, out_ref, sibling)
+
+    def to_beside(quarter, n):
+        return copy_of(2, quarter, n, out_ref, beside)
+
+    def to_outer(quarter, n):
+        return copy_of(3, quarter, n, out_ref, outer)
+
+    def role(core, half):
+        mine = [2 * half + core] if split else [core, 2 + core]
+        nexts = [2 * (1 - half) + core] if split else []
+        theirs = [1 - core, 3 - core]
+        order = [(quarter, n) for n in range(count) for quarter in mine]
+
+        def send_all():
+            for quarter, n in order:
+                cross(quarter, n).start()
+
+        if relay:
+            pl.when(inner)(send_all)
+        else:
+            send_all()
+        for n in range(count):
+            for quarter in mine:
+                cross(quarter, n).wait_recv()
+                if relay:
+
+                    @pl.when(inner)
+                    def _():
+                        to_outer(quarter, n).start()
+
+                if split:
+                    to_beside(quarter, n).start()
+                to_sibling(quarter, n).start()
+            for quarter in mine:
+                mirror(quarter, n)
+            if n:
+                for quarter in nexts:
+                    to_beside(quarter, n - 1).wait_recv()
+                    to_sibling(quarter, n - 1).start()
+                    mirror(quarter, n - 1)
+            if n > 1:
+                for quarter in theirs:
+                    to_sibling(quarter, n - 2).wait_recv()
+                    mirror(quarter, n - 2)
+        for quarter in nexts:
+            to_beside(quarter, count - 1).wait_recv()
+            to_sibling(quarter, count - 1).start()
+            mirror(quarter, count - 1)
+        for n in range(count - 2, count):
+            for quarter in theirs:
+                to_sibling(quarter, n).wait_recv()
+                mirror(quarter, n)
+
+        def crossed():
+            for quarter, n in order:
+                cross(quarter, n).wait_send()
+                if relay:
+                    to_outer(quarter, n).wait_send()
+
+        if relay:
+            pl.when(inner)(crossed)
+        else:
+            crossed()
+        for n in range(count):
+            for quarter in mine:
+                if split:
+                    to_beside(quarter, n).wait_send()
+            for quarter in mine + nexts:
+                to_sibling(quarter, n).wait_send()
 
     for core in range(2):
-
-        @pl.when(col == core)
-        def _():
-            sends, forwards = [], []
-            for i in orders[core]:
-                copy = pltpu.make_async_remote_copy(
-                    src_ref=strip_of(c_ref, i),
-                    dst_ref=strip_of(land, i),
-                    send_sem=send_sem.at[i],
-                    recv_sem=recv_sem.at[i],
-                    device_id=(partner, col),
-                    device_id_type=MESH,
-                )
-                copy.start()
-                sends.append(copy)
-            theirs = []
-            for i in orders[1 - core]:
-                theirs.append(
-                    pltpu.make_async_remote_copy(
-                        src_ref=strip_of(land, i),
-                        dst_ref=strip_of(land, i),
-                        send_sem=fsend_sem.at[i],
-                        recv_sem=frecv_sem.at[i],
-                        device_id=(leaf, 1 - col),
-                        device_id_type=MESH,
-                    )
-                )
-            for n, i in enumerate(orders[core]):
-                sends[n].wait_recv()
-                forward = pltpu.make_async_remote_copy(
-                    src_ref=strip_of(land, i),
-                    dst_ref=strip_of(land, i),
-                    send_sem=fsend_sem.at[i],
-                    recv_sem=frecv_sem.at[i],
-                    device_id=(leaf, 1 - col),
-                    device_id_type=MESH,
-                )
-                forward.start()
-                forwards.append(forward)
-                out_ref[i * T : (i + 1) * T, : (i + 1) * T] = land[
-                    i * T : (i + 1) * T, : (i + 1) * T
-                ]
-                mirror_strip(out_ref, i)
-                if n:
-                    j = orders[1 - core][n - 1]
-                    theirs[n - 1].wait_recv()
-                    out_ref[j * T : (j + 1) * T, : (j + 1) * T] = land[
-                        j * T : (j + 1) * T, : (j + 1) * T
-                    ]
-                    mirror_strip(out_ref, j)
-            j = orders[1 - core][-1]
-            theirs[-1].wait_recv()
-            out_ref[j * T : (j + 1) * T, : (j + 1) * T] = land[
-                j * T : (j + 1) * T, : (j + 1) * T
-            ]
-            mirror_strip(out_ref, j)
-            for copy in sends + forwards:
-                copy.wait_send()
+        for half in range(2) if split else [0]:
+            chosen = (col == core) & (side == half) if split else col == core
+            pl.when(chosen)(functools.partial(role, core, half))
 
 
 def exchange(current, level, collective):
@@ -187,8 +266,10 @@
         out_shape=jax.ShapeDtypeStruct((width, width), F32),
         in_specs=[pl.BlockSpec(memory_space=pltpu.VMEM)],
         out_specs=pl.BlockSpec(memory_space=pltpu.VMEM),
-        scratch_shapes=[pltpu.VMEM((width, width), F32)]
-        + [pltpu.SemaphoreType.DMA((strips,)) for _ in range(4)],
+        scratch_shapes=[
+            pltpu.SemaphoreType.DMA((4, 4, len(pieces_of(0, strips)))),
+            pltpu.SemaphoreType.DMA((4, len(pieces_of(0, strips)))),
+        ],
         compiler_params=pltpu.CompilerParams(
             collective_id=collective, has_side_effects=True, vmem_limit_bytes=VMEM_BYTES
         ),
@@ -226,16 +307,17 @@
 
 
 def front_kernel(
-    strips, last, idx_ref, own_ref, other_ref, factor_ref, next_ref, front, work, upper, low, u, uh, ul
+    level, last, idx_ref, own_ref, other_ref, factor_ref, next_ref, front, work, upper, low, u, uh, ul, *full
 ):
+    width = own_ref.shape[0]
+    groups = width // G
     subs = front.shape[0] // SB
     per = T // SB
     pivot_tiles = KP // T
-    tiles = front.shape[1] // T
     lane_group = lax.broadcasted_iota(jnp.int32, (SB, T), 1) // SB
 
     def entry(child, field, s):
-        return idx_ref[(child * 5 + field) * subs + s]
+        return idx_ref[((level * 2 + child) * 5 + field) * subs + s]
 
     def assemble(r, tile_count):
         base = pl.multiple_of(r * SB, SB)
@@ -273,9 +355,11 @@
     def _(r):
         assemble(r, pivot_tiles)
 
-    @pl.loop(KP // SB, subs)
-    def _(r):
-        assemble(r, tiles)
+    for g in range(groups):
+
+        @pl.loop((KP + g * G) // SB, (KP + (g + 1) * G) // SB)
+        def _(r):
+            assemble(r, (KP + (g + 1) * G) // T)
 
     work[...] = front[:KP, :KP]
     lanes = lax.broadcasted_iota(jnp.int32, (NB, KP), 1)
@@ -311,36 +395,36 @@
     factor_ref[:share, :] = work[pl.ds(pl.multiple_of(col * share, share), share), :]
     inverse = split2(low[...])
 
-    @pl.loop(0, strips)
-    def _(i):
-        base = pl.multiple_of(i * T, T)
-        coupling = front[pl.ds(pl.multiple_of(KP + base, T), T), :KP]
-        strip = dot3(split2(coupling), inverse, ((1,), (1,)))
-        u[pl.ds(base, T), :] = strip
-        hi, lo = split2(strip)
-        uh[pl.ds(base, T), :] = hi
-        ul[pl.ds(base, T), :] = lo
-
-    half = strips * T // 2
-    factor_ref[share:, :] = u[pl.ds(pl.multiple_of(col * half, half), half), :]
-    offset = col * half if last else 0
-    whole = (uh[...], ul[...])
-
-    @pl.loop(0, strips // 2 if last else strips)
-    def _(i):
-        base = pl.multiple_of(i * T, T)
-        at = pl.multiple_of(base + offset, T)
-        product = dot3((uh[pl.ds(at, T), :], ul[pl.ds(at, T), :]), whole, ((1,), (1,)))
-        next_ref[pl.ds(base, T), :] = front[pl.ds(pl.multiple_of(at + KP, T), T), KP:] - product
-
-
-def merge(own, other, index, last):
+    result = full[0] if last else next_ref
+    for g in range(groups):
+        lo, hi = g * G, (g + 1) * G
+        strip = dot3(split2(front[KP + lo : KP + hi, :KP]), inverse, ((1,), (1,)))
+        u[lo:hi, :] = strip
+        uh[lo:hi, :], ul[lo:hi, :] = split2(strip)
+    for g in range(groups):
+        lo, hi = g * G, (g + 1) * G
+        product = dot3(
+            (uh[lo:hi, :], ul[lo:hi, :]), (uh[:hi, :], ul[:hi, :]), ((1,), (1,))
+        )
+        result[lo:hi, :hi] = front[KP + lo : KP + hi, KP : KP + hi] - product
+        for k in range(g):
+            result[k * G : (k + 1) * G, lo:hi] = result[lo:hi, k * G : (k + 1) * G].T
+
+    half = width // 2
+    own_half = pl.ds(pl.multiple_of(col * half, half), half)
+    factor_ref[share:, :] = u[own_half, :]
+    if last:
+        next_ref[...] = result[own_half, :]
+
+
+def merge(own, other, index, level):
     width = own.shape[0]
     front_width = width + KP
+    last = level == LEVELS - 1
     out_rows = width // 2 if last else width
     vmem = pl.BlockSpec(memory_space=pltpu.VMEM)
     return pl.pallas_call(
-        functools.partial(front_kernel, width // T, last),
+        functools.partial(front_kernel, level, last),
         out_shape=(
             jax.ShapeDtypeStruct((front_width // 2, KP), F32),
             jax.ShapeDtypeStruct((out_rows, width), F32),
@@ -355,33 +439,31 @@
             pltpu.VMEM((width, KP), F32),
             pltpu.VMEM((width, KP), BF16),
             pltpu.VMEM((width, KP), BF16),
-        ],
+        ]
+        + ([pltpu.VMEM((width, width), F32)] if last else []),
         compiler_params=pltpu.CompilerParams(vmem_limit_bytes=VMEM_BYTES),
         name="front",
     )(index, own, other)
 
 
 def index_table(child_maps, sub_count):
-    col_count, child_subs = child_maps.shape
+    col_count, child_subs = child_maps.shape[-2:]
     per = T // SB
     pivot_subs = KP // col_count // SB
-    matches = (child_maps[:, :, None] == lax.iota(jnp.int32, sub_count)[None, None, :]).astype(
-        jnp.int32
-    )
+    matches = child_maps[..., :, None] == lax.iota(jnp.int32, sub_count)
     offset = lax.iota(jnp.int32, col_count)[:, None] * child_subs
-    source = jnp.sum(matches * lax.iota(jnp.int32, child_subs)[None, :, None], axis=1) + offset
-    present = jnp.sum(matches, axis=1)
-
-    def pivots_first(table):
-        return jnp.concatenate(
-            [table[:, :pivot_subs].reshape(-1), table[:, pivot_subs:].reshape(-1)]
-        )
-
-    source, present = pivots_first(source), pivots_first(present)
-    place = lax.iota(jnp.int32, source.shape[0]) % per
+    names = lax.iota(jnp.int32, child_subs)[:, None] + 1
+    found = jnp.sum(jnp.where(matches, names, 0), axis=-2)
+    coded = jnp.where(found > 0, found + offset, 0)
+    parts = [coded[:, :, c, :pivot_subs] for c in range(col_count)]
+    parts += [coded[:, :, c, pivot_subs:] for c in range(col_count)]
+    coded = jnp.concatenate(parts, axis=-1)
+    present = (coded > 0).astype(jnp.int32)
+    source = jnp.maximum(coded - 1, 0)
+    place = lax.broadcasted_iota(jnp.int32, coded.shape, 2) % per
     shift = (place - source % per + per) % per * SB
     group = jnp.where(present > 0, place, -1)
-    return jnp.concatenate([source, present, source // per, shift, group])
+    return jnp.stack([source, present, source // per, shift, group], axis=2).reshape(-1)
 
 
 def body(rows_a, stair_counts, block_maps):
@@ -397,19 +479,17 @@
     column_block = lax.iota(jnp.int32, width) // (width // stair_counts.shape[1])
     masked = jnp.where(column_block[None, :] >= leading[:, None], rows_a, jnp.zeros_like(rows_a))
     current = gram(masked, 0)
+    chosen = []
+    for level in range(LEVELS):
+        front_maps = lax.dynamic_index_in_dim(
+            block_maps[level], leaf_index >> level + 1, 0, keepdims=False
+        )
+        chosen.append(jnp.where((leaf_index >> level & 1) == 0, front_maps, front_maps[::-1]))
+    index = index_table(jnp.stack(chosen), sub_count)
     factors = []
     for level in range(LEVELS):
         other = exchange(current, level, level + 1)
-        pair_bit = leaf_index >> level & 1
-        front_maps = lax.dynamic_index_in_dim(
-            block_maps[level], leaf_index >> level + 1, 0, keepdims=False
-        )
-        own_maps = lax.dynamic_index_in_dim(front_maps, pair_bit, 0, keepdims=False)
-        other_maps = lax.dynamic_index_in_dim(front_maps, 1 - pair_bit, 0, keepdims=False)
-        index = jnp.concatenate(
-            [index_table(own_maps, sub_count), index_table(other_maps, sub_count)]
-        )
-        factor, current = merge(current, other, index, level == LEVELS - 1)
+        factor, current = merge(current, other, index, level)
         factors.append(factor)
     return (jnp.stack(factors)[:, None], current[None])
 

time: 359 us -> 282 us (0.79)
  Pallas kernels: 335 us -> 267 us
  local copies, waits for them, and re-layouts: 7.26 us -> 1.63 us
    pallas_call x4, Pallas kernels: 163 us -> 125 us  [exchange(): pl.pallas_call(functools.partial(exchange_kernel, strips, level), out_sha...]
    pallas_call x4, Pallas kernels: 163 us -> 133 us  [merge(): pl.pallas_call(functools.partial(front_kernel, level, last), out_shape=(j...]
where the time goes in v2:
time: 282 us; the launch traced here: 277 us
  Pallas kernels  267 us (95%)
  other arithmetic  7.6 us (3%)
    pallas_call x4, Pallas kernels, merge(): pl.pallas_call(functools.partial(front_kernel, level, last), out_shape=(j...  133 us
    pallas_call x4, Pallas kernels, exchange(): pl.pallas_call(functools.partial(exchange_kernel, strips, level), out_sha...  125 us
    pallas_call x1, Pallas kernels, gram(): pl.pallas_call(functools.partial(gram_kernel, strips), out_shape=jax.Shap...  8.68 us

profile of v2, /device:TPU:0, one launch (start us, length us, event | category | flops | bytes accessed | tf_op | source)
XLA Modules:
  0.0 277.1 jit_solution(12536476669273884166)
XLA Ops:
  0.7 0.8 reduce-window.8
  1.5 0.1 convert_reduce_fusion
  1.6 0.8 fusion.10
  2.5 0.1 select_reduce_fusion
  2.6 0.1 compare_select_fusion.4
  2.7 0.1 fusion.12
  2.8 0.1 compare_select_fusion.3
  2.9 0.1 fusion.3
  3.0 0.7 reshape.353.idx_ref
  3.7 3.5 %compare_select_fusion.m_ref = bf16[1024,1024]{1,0:T(8,128)(2,1)} fusion(bf16[1024,1024]{1,0:T(8,128)(2,1)} %param.3, s32[1024]{0:T(1024)S(1)} %add_select_fusion, s32[1024]{0:T(1024)S(1)} %convert_reduce_fusion), kind=kLoop, calls=%fused_computation | loop fusion | flops 2097152 | bytes 4202496 | tf_op jit(solution)/shard_map/jit(_where)/select_n | solution.py:480
  7.2 8.7 %gram.1.c_ref.own_ref = f32[1024,1024]{1,0:T(8,128)} custom-call(bf16[1024,1024]{1,0:T(8,128)(2,1)} %compare_select_fusion.m_ref), custom_call_target="tpu_custom_call" | custom-call | tf_op jit(solution)/shard_map/gram/pallas_call | solution.py:91
  15.8 35.6 %exchange.4.other_ref = f32[1024,1024]{1,0:T(8,128)} custom-call(f32[1024,1024]{1,0:T(8,128)} %gram.1.c_ref.own_ref), custom_call_target="tpu_custom_call" | custom-call | tf_op jit(solution)/shard_map/exchange/pallas_call | solution.py:264
  51.5 33.2 %front.4 = (f32[640,256]{1,0:T(8,128)}, f32[1024,1024]{1,0:T(8,128)}) custom-call(s32[1600]{0:T(1024)} %reshape.353.idx_ref, f32[1024,1024]{1,0:T(8,128)} %gram.1.c_ref.own_ref, f32[1024,1024]{1,0:T(8,128)} %exchange.4.other_ref), custom_call_target="tpu_custom_call" | custom-call | tf_op jit(solution)/shard_map/front/pallas_call | solution.py:426
  84.6 27.7 %exchange.5.other_ref = f32[1024,1024]{1,0:T(8,128)} custom-call(f32[1024,1024]{1,0:T(8,128)} %get-tuple-element.11.c_ref.own_ref), custom_call_target="tpu_custom_call" | custom-call | tf_op jit(solution)/shard_map/exchange/pallas_call | solution.py:264
  112.3 33.3 %front.5 = (f32[640,256]{1,0:T(8,128)}, f32[1024,1024]{1,0:T(8,128)}) custom-call(s32[1600]{0:T(1024)} %reshape.353.idx_ref, f32[1024,1024]{1,0:T(8,128)} %get-tuple-element.11.c_ref.own_ref, f32[1024,1024]{1,0:T(8,128)} %exchange.5.other_ref), custom_call_target="tpu_custom_call" | custom-call | tf_op jit(solution)/shard_map/front/pallas_call | solution.py:426
  145.6 27.7 %exchange.6.other_ref = f32[1024,1024]{1,0:T(8,128)} custom-call(f32[1024,1024]{1,0:T(8,128)} %get-tuple-element.13.c_ref.own_ref), custom_call_target="tpu_custom_call" | custom-call | tf_op jit(solution)/shard_map/exchange/pallas_call | solution.py:264
  173.3 33.3 %front.6 = (f32[640,256]{1,0:T(8,128)}, f32[1024,1024]{1,0:T(8,128)}) custom-call(s32[1600]{0:T(1024)} %reshape.353.idx_ref, f32[1024,1024]{1,0:T(8,128)} %get-tuple-element.13.c_ref.own_ref, f32[1024,1024]{1,0:T(8,128)} %exchange.6.other_ref), custom_call_target="tpu_custom_call" | custom-call | tf_op jit(solution)/shard_map/front/pallas_call | solution.py:426
  206.6 33.8 %exchange.7.other_ref = f32[1024,1024]{1,0:T(8,128)} custom-call(f32[1024,1024]{1,0:T(8,128)} %get-tuple-element.15.c_ref.own_ref), custom_call_target="tpu_custom_call" | custom-call | tf_op jit(solution)/shard_map/exchange/pallas_call | solution.py:264
  240.4 0.0 copy-start
  240.4 0.0 copy-start.1
  240.4 0.0 copy-start.2
  240.4 33.7 %front.7 = (f32[640,256]{1,0:T(8,128)}, f32[512,1024]{1,0:T(8,128)}) custom-call(s32[1600]{0:T(1024)} %reshape.353.idx_ref, f32[1024,1024]{1,0:T(8,128)} %get-tuple-element.15.c_ref.own_ref, f32[1024,1024]{1,0:T(8,128)} %exchange.7.other_ref), custom_call_target="tpu_custom_call" | custom-call | tf_op jit(solution)/shard_map/front/pallas_call | solution.py:426
  274.1 0.0 copy-done
  274.1 0.0 copy-done.1
  274.1 0.0 copy-done.2
  274.1 2.8 %maximum_bitcast_fusion = f32[4,1,640,256]{3,2,1,0:T(8,128)} fusion(f32[1,640,256]{2,1,0:T(8,128)} %bitcast.30, f32[1,640,256]{2,1,0:T(8,128)S(1)} %bitcast.29, f32[1,640,256]{2,1,0:T(8,128)S(1)} %bitcast.28, f32[1,640,256]{2,1,0:T(8,128)S(1)} %bitcast.27), kind=kLoop, calls=%fused_computation.1 | loop fusion | flops 1966080 | bytes 5242880
  (16 shorter events, 0.1 us)
Async XLA Ops:
  240.4 33.7 %copy-start = (f32[640,256]{1,0:T(8,128)S(1)}, f32[640,256]{1,0:T(8,128)}, u32[]{:S(2)}) copy-start(f32[640,256]{1,0:T(8,128)} %get-tuple-element.10) | copy-start | bytes 1966084
  240.4 33.7 %copy-start.1 = (f32[640,256]{1,0:T(8,128)S(1)}, f32[640,256]{1,0:T(8,128)}, u32[]{:S(2)}) copy-start(f32[640,256]{1,0:T(8,128)} %get-tuple-element.12) | copy-start | bytes 1966084
  240.4 33.7 %copy-start.2 = (f32[640,256]{1,0:T(8,128)S(1)}, f32[640,256]{1,0:T(8,128)}, u32[]{:S(2)}) copy-start(f32[640,256]{1,0:T(8,128)} %get-tuple-element.14) | copy-start | bytes 1966084
